TPU v7x, 32 devices: a whole 2x2x4 slice. The times are simulated.
32 devices in a mesh: lev: 4 (over x, core), lon: 8 (over z, y).
Axes of the slice: x: 2, y: 2, z: 4, core: 2. Of those that a mesh axis runs over, the one named last changes fastest.
Arguments:
- wave_state: float32 [3, 128, 8, 2048], P(None, 'lev', None, 'lon'), may hold values from -6 to 6
- to_modes: float32 [128, 128], replicated, may hold values from -1 to 2.5
- from_modes: float32 [128, 128], replicated, may hold values from -1 to 2.5
- courant: float32 [128], P('lev'), may hold values from 0.25 to 4
- shifts: float32 [3], replicated, may hold values from 0.5 to 2
Outputs:
- advanced: float32 [3, 128, 8, 2048], P(None, 'lev', None, 'lon')
All inputs are finite; a program needn't handle non-finite values.
Results may differ from a plain program's by a relative error of at most 0.004.
Values sent between devices are 32-bit elements; how exact they have to be, the bound alone decides.
A program may use at most 64 MiB of HBM per device.

v0:
```python
import math

import jax
import jax.numpy as jnp
from jax import lax
from jax.sharding import PartitionSpec as P

KDIM = 4
SWEEPS = 3
SQUARINGS = 16
TAYLOR = 8


highest = lax.Precision.HIGHEST
epsilon = 1e-06


def from_behind(value, axis, steps):
    count = lax.axis_size(axis)
    pairs = [(source, (source + steps) % count) for source in range(count)]
    return lax.ppermute(value, axis, pairs)


def geometry(lon_cells, rows):
    spacing = 2.0 * math.pi / lon_cells
    row_index = jnp.arange(rows, dtype=jnp.float32)
    centre = jnp.sin((row_index + 0.5) * spacing)
    face_sin = jnp.where(row_index < rows - 1, jnp.sin((row_index + 1.0) * spacing), 0.0)
    face_below = jnp.concatenate([jnp.zeros((1,), jnp.float32), face_sin[:-1]])
    return (centre[:, None], face_sin[:, None], face_below[:, None])


def geometric_run(values, decay_rate, reverse):
    length = values.shape[-1]
    result = values
    stride = 1
    while stride < length:
        factor = jnp.exp(-decay_rate * stride)
        if reverse:
            shifted = jnp.concatenate(
                [result[..., stride:], jnp.zeros_like(result[..., :stride])], axis=-1
            )
        else:
            shifted = jnp.concatenate(
                [jnp.zeros_like(result[..., :stride]), result[..., :-stride]], axis=-1
            )
        result = result + factor * shifted
        stride = stride * 2
    return result


def line_terms(courant, shift_value, geometry_terms):
    centre, face_sin, face_below = geometry_terms
    wave_speed = courant[:, None, None]
    zonal_coef = wave_speed / (centre * centre)
    merid_diag = wave_speed * (face_sin + face_below) / centre
    half_ratio = 0.5 * (shift_value * shift_value + merid_diag) / zonal_coef
    decay_rate = jnp.log1p(half_ratio + jnp.sqrt(half_ratio * (half_ratio + 2.0)))
    return (zonal_coef, decay_rate)


def incoming(gathered, decay_rate, cell_count, denom, reverse):
    cycle_size = gathered.shape[0]
    my_index = lax.axis_index("lon")
    all_index = jnp.arange(cycle_size, dtype=jnp.int32)
    if reverse:
        distance = (all_index - my_index - 1) % cycle_size
    else:
        distance = (my_index - 1 - all_index) % cycle_size
    spans = (cell_count * distance.astype(jnp.float32))[:, None, None]
    weight = jnp.exp(-decay_rate[None, :, :, 0] * spans)
    return jnp.sum(gathered * weight, axis=0) / denom[:, :, 0]


def line_inverse(right_side, zonal_coef, decay_rate):
    cell_count = right_side.shape[-1]
    position = jnp.arange(cell_count, dtype=jnp.float32)
    denom = -jnp.expm1(-decay_rate * (cell_count * lax.axis_size("lon")))
    rising = jnp.exp(-decay_rate * (position + 1.0))
    falling = jnp.exp(-decay_rate * (cell_count - position))
    ahead = geometric_run(right_side, decay_rate, False)
    behind = geometric_run(right_side, decay_rate, True)
    ends_ahead, ends_behind = (
        lax.all_gather(ahead[..., -1][None], "lon", axis=0, tiled=True),
        lax.all_gather(behind[..., 0][None], "lon", axis=0, tiled=True),
    )
    ahead = ahead + rising * incoming(ends_ahead, decay_rate, cell_count, denom, False)[..., None]
    behind = (
        behind + falling * incoming(ends_behind, decay_rate, cell_count, denom, True)[..., None]
    )
    joined = (ahead + behind - right_side) / -jnp.expm1(-2.0 * decay_rate)
    return jnp.exp(-decay_rate) / zonal_coef * joined


def north_diff(values):
    return jnp.concatenate(
        [values[..., 1:, :] - values[..., :-1, :], jnp.zeros_like(values[..., :1, :])], axis=-2
    )


def divergence(east_wind, west_wind, north_wind, geometry_terms):
    centre, face_sin, face_below = geometry_terms
    flux = face_sin * north_wind
    below = jnp.concatenate([jnp.zeros_like(flux[..., :1, :]), flux[..., :-1, :]], axis=-2)
    return (east_wind - west_wind) / centre + (flux - below) / centre


def coupling(values, geometry_terms):
    centre, face_sin, face_below = geometry_terms
    upper = jnp.concatenate([values[..., 1:, :], jnp.zeros_like(values[..., :1, :])], axis=-2)
    lower = jnp.concatenate([jnp.zeros_like(values[..., :1, :]), values[..., :-1, :]], axis=-2)
    return (face_sin * upper + face_below * lower) / centre


def apply_operator(vector, west_u, east_p, courant, geometry_terms):
    centre = geometry_terms[0]
    wave_speed = courant[:, None, None]
    new_east = -(east_p - vector[2]) / centre
    new_north = -north_diff(vector[2])
    new_height = -wave_speed * divergence(vector[0], west_u, vector[1], geometry_terms)
    return jnp.stack([new_east, new_north, new_height])


def inner_product(first_vec, second_vec, courant, geometry_terms):
    centre, face_sin, face_below = geometry_terms
    weighted = centre * first_vec[0] * second_vec[0] + face_sin * first_vec[1] * second_vec[1]
    weighted = weighted + centre / courant[:, None, None] * first_vec[2] * second_vec[2]
    return jnp.sum(weighted, axis=(-2, -1))


def exponential(matrix):
    dimension = matrix.shape[-1]
    identity = jnp.eye(dimension, dtype=matrix.dtype)
    scaled = matrix / float(2**SQUARINGS)
    result = jnp.broadcast_to(identity, matrix.shape)
    for degree in range(TAYLOR, 0, -1):
        result = identity + jnp.einsum("mij,mjk->mik", scaled, result, precision=highest) / degree
    for repeat in range(SQUARINGS):
        result = jnp.einsum("mij,mjk->mik", result, result, precision=highest)
    return result


def edge_column(column, offset):
    return from_behind(column, "lon", offset)


def lon_total(values):
    return lax.psum(values, "lon")


def shifted_solve(vector, courant, shift_value, geometry_terms):
    wave_speed = courant[:, None, None]
    west_u = jnp.concatenate([edge_column(vector[0][..., -1:], 1), vector[0][..., :-1]], axis=-1)
    right_side = shift_value * vector[2] - wave_speed * divergence(
        vector[0], west_u, vector[1], geometry_terms
    )
    zonal_coef, decay_rate = line_terms(courant, shift_value, geometry_terms)
    solved = jnp.zeros_like(right_side)
    for sweep_no in range(SWEEPS):
        source = right_side + wave_speed * coupling(solved, geometry_terms)
        solved = line_inverse(source, zonal_coef, decay_rate)
    east_p = jnp.concatenate([solved[..., 1:], edge_column(solved[..., :1], -1)], axis=-1)
    new_east = (vector[0] - (east_p - solved) / geometry_terms[0]) / shift_value
    new_north = (vector[1] - north_diff(solved)) / shift_value
    return jnp.stack([new_east, new_north, solved])


def advance_modes(modal_fields, courant, shifts, geometry_terms):
    start_norm = jnp.sqrt(
        lon_total(inner_product(modal_fields, modal_fields, courant, geometry_terms)) + epsilon
    )
    krylov_basis = [modal_fields / start_norm[:, None, None]]
    for step_no in range(1, KDIM):
        candidate = shifted_solve(krylov_basis[-1], courant, shifts[step_no - 1], geometry_terms)
        projections = lon_total(
            jnp.stack(
                [
                    inner_product(earlier, candidate, courant, geometry_terms)
                    for earlier in krylov_basis
                ]
            )
        )
        for number, earlier in enumerate(krylov_basis):
            candidate = candidate - projections[number][:, None, None] * earlier
        new_norm = jnp.sqrt(
            lon_total(inner_product(candidate, candidate, courant, geometry_terms)) + epsilon
        )
        krylov_basis.append(candidate / new_norm[:, None, None])
    west_cols = edge_column(jnp.stack([vec[0][..., -1:] for vec in krylov_basis]), 1)
    east_cols = edge_column(jnp.stack([vec[2][..., :1] for vec in krylov_basis]), -1)
    images = []
    for number, column_vec in enumerate(krylov_basis):
        west_u = jnp.concatenate([west_cols[number], column_vec[0][..., :-1]], axis=-1)
        east_p = jnp.concatenate([column_vec[2][..., 1:], east_cols[number]], axis=-1)
        images.append(apply_operator(column_vec, west_u, east_p, courant, geometry_terms))
    local_matrix = jnp.stack(
        [
            jnp.stack(
                [inner_product(row_vec, image, courant, geometry_terms) for image in images],
                axis=-1,
            )
            for row_vec in krylov_basis
        ],
        axis=-2,
    )
    reduced = lon_total(local_matrix)
    skew_part = 0.5 * (reduced - jnp.swapaxes(reduced, -1, -2))
    propagator = exponential(skew_part)
    mixing = start_norm[:, None] * propagator[:, :, 0]
    result = mixing[:, 0][:, None, None] * krylov_basis[0]
    for number in range(1, KDIM):
        result = result + mixing[:, number][:, None, None] * krylov_basis[number]
    return result


def regroup(fields, matrix):
    mixed = jnp.einsum(
        "ml,flac->fmac",
        matrix,
        lax.all_to_all(fields, "lev", split_axis=3, concat_axis=1, tiled=True),
        precision=highest,
    )
    return lax.all_to_all(mixed, "lev", split_axis=1, concat_axis=3, tiled=True)


def body(wave_state, to_modes, from_modes, courant, shifts):
    cell_count = wave_state.shape[-1]
    geometry_terms = geometry(cell_count * lax.axis_size("lon"), wave_state.shape[2])
    modal_fields = regroup(wave_state, to_modes)
    advanced_modal = advance_modes(modal_fields, courant, shifts, geometry_terms)
    return regroup(advanced_modal, from_modes)


def solution(mesh):
    in_specs = (P(None, "lev", None, "lon"), P(), P(), P("lev"), P())
    out_specs = P(None, "lev", None, "lon")
    return jax.shard_map(body, mesh=mesh, in_specs=in_specs, out_specs=out_specs, check_vma=False)
```

profile of v0, /device:TPU:0, one launch (start us, length us, event | category | flops | bytes accessed | tf_op | source)
XLA Modules:
  0.0 1044.4 jit_solution(3039104126975685439)
XLA Ops:
  66.5 22.4 %psum.56 = f32[32]{0:T(128)S(1)} all-reduce(f32[32]{0:T(128)S(1)} %fusion.12), channel_id=1, replica_groups=mesh['lev'=4,'lon'=8] {'lon'}, use_global_device_ids=true, to_apply=%region_1.2 | all-reduce | flops 32 | bytes 256 | tf_op jit(solution)/shard_map/psum | solution.py:148
  105.6 30.5 %all-gather = f32[256,8,1]{1,2,0:T(1,128)S(1)} all-gather(f32[32,8,1]{1,2,0:T(1,128)S(1)} %copy.1769), channel_id=2, replica_groups=mesh['lev'=4,'lon'=8] {'lon'}, dimensions={0}, use_global_device_ids=true | all-gather | bytes 9216 | tf_op jit(solution)/shard_map/all_gather | solution.py:84
  136.5 30.5 %all-gather.1 = f32[256,8,1]{1,2,0:T(1,128)S(1)} all-gather(f32[32,8,1]{1,2,0:T(1,128)S(1)} %copy.1772), channel_id=3, replica_groups=mesh['lev'=4,'lon'=8] {'lon'}, dimensions={0}, use_global_device_ids=true | all-gather | bytes 9216 | tf_op jit(solution)/shard_map/all_gather | solution.py:85
  173.7 30.5 %all-gather.2 = f32[256,8,1]{1,2,0:T(1,128)S(1)} all-gather(f32[32,8,1]{1,2,0:T(1,128)S(1)} %copy.1776), channel_id=4, replica_groups=mesh['lev'=4,'lon'=8] {'lon'}, dimensions={0}, use_global_device_ids=true | all-gather | bytes 9216 | tf_op jit(solution)/shard_map/all_gather | solution.py:84
  204.6 30.7 %all-gather.3 = f32[256,8,1]{1,2,0:T(1,128)S(1)} all-gather(f32[32,8,1]{1,2,0:T(1,128)S(1)} %copy.1779), channel_id=5, replica_groups=mesh['lev'=4,'lon'=8] {'lon'}, dimensions={0}, use_global_device_ids=true | all-gather | bytes 9216 | tf_op jit(solution)/shard_map/all_gather | solution.py:85
  242.0 30.5 %all-gather.4 = f32[256,8,1]{1,2,0:T(1,128)S(1)} all-gather(f32[32,8,1]{1,2,0:T(1,128)S(1)} %copy.1782), channel_id=6, replica_groups=mesh['lev'=4,'lon'=8] {'lon'}, dimensions={0}, use_global_device_ids=true | all-gather | bytes 9216 | tf_op jit(solution)/shard_map/all_gather | solution.py:84
  272.9 30.5 %all-gather.5 = f32[256,8,1]{1,2,0:T(1,128)S(1)} all-gather(f32[32,8,1]{1,2,0:T(1,128)S(1)} %copy.1785), channel_id=7, replica_groups=mesh['lev'=4,'lon'=8] {'lon'}, dimensions={0}, use_global_device_ids=true | all-gather | bytes 9216 | tf_op jit(solution)/shard_map/all_gather | solution.py:85
  310.5 20.0 %psum.57 = f32[32]{0:T(128)S(1)} all-reduce(f32[32]{0:T(128)S(1)} %get-tuple-element.61), channel_id=1, replica_groups=mesh['lev'=4,'lon'=8] {'lon'}, use_global_device_ids=true, to_apply=%region_9.10 | all-reduce | flops 32 | bytes 256 | tf_op jit(solution)/shard_map/psum | solution.py:148
  331.3 17.1 %psum.58 = f32[32]{0:T(128)S(1)} all-reduce(f32[32]{0:T(128)S(1)} %fusion.15), channel_id=1, replica_groups=mesh['lev'=4,'lon'=8] {'lon'}, use_global_device_ids=true, to_apply=%region_11.12 | all-reduce | flops 32 | bytes 256 | tf_op jit(solution)/shard_map/psum | solution.py:148
  366.2 30.8 %all-gather.6 = f32[256,8,1]{1,2,0:T(1,128)S(1)} all-gather(f32[32,8,1]{1,2,0:T(1,128)} %copy.1800), channel_id=8, replica_groups=mesh['lev'=4,'lon'=8] {'lon'}, dimensions={0}, use_global_device_ids=true | all-gather | bytes 9216 | tf_op jit(solution)/shard_map/all_gather | solution.py:84
  399.4 30.8 %all-gather.7 = f32[256,8,1]{1,2,0:T(1,128)S(1)} all-gather(f32[32,8,1]{1,2,0:T(1,128)} %copy.1803), channel_id=9, replica_groups=mesh['lev'=4,'lon'=8] {'lon'}, dimensions={0}, use_global_device_ids=true | all-gather | bytes 9216 | tf_op jit(solution)/shard_map/all_gather | solution.py:85
  440.3 30.7 %all-gather.8 = f32[256,8,1]{1,2,0:T(1,128)S(1)} all-gather(f32[32,8,1]{1,2,0:T(1,128)} %copy.1807), channel_id=10, replica_groups=mesh['lev'=4,'lon'=8] {'lon'}, dimensions={0}, use_global_device_ids=true | all-gather | bytes 9216 | tf_op jit(solution)/shard_map/all_gather | solution.py:84
  473.5 31.2 %all-gather.9 = f32[256,8,1]{1,2,0:T(1,128)S(1)} all-gather(f32[32,8,1]{1,2,0:T(1,128)} %copy.1810), channel_id=11, replica_groups=mesh['lev'=4,'lon'=8] {'lon'}, dimensions={0}, use_global_device_ids=true | all-gather | bytes 9216 | tf_op jit(solution)/shard_map/all_gather | solution.py:85
  514.4 30.7 %all-gather.10 = f32[256,8,1]{1,2,0:T(1,128)S(1)} all-gather(f32[32,8,1]{1,2,0:T(1,128)} %copy.1813), channel_id=12, replica_groups=mesh['lev'=4,'lon'=8] {'lon'}, dimensions={0}, use_global_device_ids=true | all-gather | bytes 9216 | tf_op jit(solution)/shard_map/all_gather | solution.py:84
  546.7 30.9 %all-gather.11 = f32[256,8,1]{1,2,0:T(1,128)S(1)} all-gather(f32[32,8,1]{1,2,0:T(1,128)} %copy.1816), channel_id=13, replica_groups=mesh['lev'=4,'lon'=8] {'lon'}, dimensions={0}, use_global_device_ids=true | all-gather | bytes 9216 | tf_op jit(solution)/shard_map/all_gather | solution.py:85
  588.8 21.3 %psum.59 = f32[2,32]{1,0:T(2,128)S(1)} all-reduce(f32[2,32]{1,0:T(2,128)S(1)} %pad_maximum_fusion.4), channel_id=1, replica_groups=mesh['lev'=4,'lon'=8] {'lon'}, use_global_device_ids=true, to_apply=%region_20.21 | all-reduce | flops 64 | bytes 512 | tf_op jit(solution)/shard_map/psum | solution.py:148
  649.3 30.7 %all-gather.12 = f32[256,8,1]{1,2,0:T(1,128)S(1)} all-gather(f32[32,8,1]{1,2,0:T(1,128)} %copy.1830), channel_id=14, replica_groups=mesh['lev'=4,'lon'=8] {'lon'}, dimensions={0}, use_global_device_ids=true | all-gather | bytes 9216 | tf_op jit(solution)/shard_map/all_gather | solution.py:84
  682.5 30.7 %all-gather.13 = f32[256,8,1]{1,2,0:T(1,128)S(1)} all-gather(f32[32,8,1]{1,2,0:T(1,128)} %copy.1833), channel_id=15, replica_groups=mesh['lev'=4,'lon'=8] {'lon'}, dimensions={0}, use_global_device_ids=true | all-gather | bytes 9216 | tf_op jit(solution)/shard_map/all_gather | solution.py:85
  723.7 30.7 %all-gather.14 = f32[256,8,1]{1,2,0:T(1,128)S(1)} all-gather(f32[32,8,1]{1,2,0:T(1,128)} %copy.1837), channel_id=16, replica_groups=mesh['lev'=4,'lon'=8] {'lon'}, dimensions={0}, use_global_device_ids=true | all-gather | bytes 9216 | tf_op jit(solution)/shard_map/all_gather | solution.py:84
  756.9 30.9 %all-gather.15 = f32[256,8,1]{1,2,0:T(1,128)S(1)} all-gather(f32[32,8,1]{1,2,0:T(1,128)} %copy.1840), channel_id=17, replica_groups=mesh['lev'=4,'lon'=8] {'lon'}, dimensions={0}, use_global_device_ids=true | all-gather | bytes 9216 | tf_op jit(solution)/shard_map/all_gather | solution.py:85
  798.2 30.7 %all-gather.16 = f32[256,8,1]{1,2,0:T(1,128)S(1)} all-gather(f32[32,8,1]{1,2,0:T(1,128)} %copy.1843), channel_id=18, replica_groups=mesh['lev'=4,'lon'=8] {'lon'}, dimensions={0}, use_global_device_ids=true | all-gather | bytes 9216 | tf_op jit(solution)/shard_map/all_gather | solution.py:84
  831.4 30.7 %all-gather.17 = f32[256,8,1]{1,2,0:T(1,128)S(1)} all-gather(f32[32,8,1]{1,2,0:T(1,128)} %copy.1846), channel_id=19, replica_groups=mesh['lev'=4,'lon'=8] {'lon'}, dimensions={0}, use_global_device_ids=true | all-gather | bytes 9216 | tf_op jit(solution)/shard_map/all_gather | solution.py:85
  873.7 22.3 %psum.61 = f32[3,32]{1,0:T(4,128)S(1)} all-reduce(f32[3,32]{1,0:T(4,128)S(1)} %pad_maximum_fusion.3), channel_id=1, replica_groups=mesh['lev'=4,'lon'=8] {'lon'}, use_global_device_ids=true, to_apply=%region_32.33 | all-reduce | flops 96 | bytes 768 | tf_op jit(solution)/shard_map/psum | solution.py:148
  950.5 21.9 %psum.63 = f32[32,4,4]{0,2,1:T(4,128)S(1)} all-reduce(f32[32,4,4]{0,2,1:T(4,128)S(1)} %pad_maximum_fusion.2), channel_id=1, replica_groups=mesh['lev'=4,'lon'=8] {'lon'}, use_global_device_ids=true, to_apply=%region_51.52 | all-reduce | flops 512 | bytes 4096 | tf_op jit(solution)/shard_map/psum | solution.py:148
  (823 shorter events, 358.2 us)
Async XLA Ops:
  7.6 16.0 %all-to-all-start = ((f32[4,1,49152]{2,1,0:T(1,128)}), f32[4,1,49152]{2,1,0:T(1,128)S(1)}, u32[]{:S(2)}, u32[]{:S(2)}) async-start(f32[4,1,49152]{2,1,0:T(1,128)} %reshape.3543), calls=%async_computation | async-start | bytes 1572864 | tf_op jit(solution)/shard_map/all_to_all | solution.py:220
  16.5 332.2 %copy-start.60 = (f32[8]{0:T(128)}, f32[8]{0:T(128)S(1)}, u32[]{:S(2)}) copy-start(f32[8]{0:T(128)S(1)} %compare_select_fusion.4) | copy-start | bytes 100
  16.6 314.2 %copy-start.52 = (f32[8]{0:T(128)}, f32[8]{0:T(128)S(1)}, u32[]{:S(2)}) copy-start(f32[8]{0:T(128)S(1)} %get-tuple-element.322) | copy-start | bytes 100
  16.7 44.8 %copy-start.145 = (f32[8]{0:T(128)}, f32[8]{0:T(128)S(1)}, u32[]{:S(2)}) copy-start(f32[8]{0:T(128)S(1)} %get-tuple-element.64) | copy-start | bytes 100
  37.1 25.0 %all-to-all-start.1 = ((f32[4,1,49152]{2,1,0:T(1,128)}), f32[4,1,49152]{2,1,0:T(1,128)S(1)}, u32[]{:S(2)}, u32[]{:S(2)}) async-start(f32[4,1,49152]{2,1,0:T(1,128)} %reshape.3545), calls=%async_computation.1 | async-start | bytes 1572864 | tf_op jit(solution)/shard_map/all_to_all | solution.py:223
  93.7 7.7 collective-permute-start
  136.2 33.6 %copy-start.146 = (f32[8]{0:T(128)S(1)}, f32[8]{0:T(128)}, u32[]{:S(2)}) copy-start(f32[8]{0:T(128)} %copy-done.145) | copy-start | bytes 100
  204.2 33.9 %copy-start.147 = (f32[8]{0:T(128)S(1)}, f32[8]{0:T(128)}, u32[]{:S(2)}) copy-start(f32[8]{0:T(128)} %copy-done.145) | copy-start | bytes 100
  241.2 62.3 %copy-start.141 = (f32[8]{0:T(128)S(1)}, f32[8]{0:T(128)}, u32[]{:S(2)}) copy-start(f32[8]{0:T(128)} %get-tuple-element.325) | copy-start | bytes 100
  241.2 62.3 %copy-start.142 = (f32[8]{0:T(128)S(1)}, f32[8]{0:T(128)}, u32[]{:S(2)}) copy-start(f32[8]{0:T(128)} %get-tuple-element.326) | copy-start | bytes 100
  241.2 62.4 %copy-start.140 = (f32[8]{0:T(128)S(1)}, f32[8]{0:T(128)}, u32[]{:S(2)}) copy-start(f32[8]{0:T(128)} %copy-done.139) | copy-start | bytes 100
  241.2 62.4 %copy-start.144 = (f32[8]{0:T(128)S(1)}, f32[8]{0:T(128)}, u32[]{:S(2)}) copy-start(f32[8]{0:T(128)} %copy-done.143) | copy-start | bytes 100
  241.2 62.7 %copy-start.136 = (f32[256]{0:T(256)S(1)}, f32[256]{0:T(256)}, u32[]{:S(2)}) copy-start(f32[256]{0:T(256)} %get-tuple-element.327) | copy-start | bytes 3076
  241.2 62.7 %copy-start.137 = (f32[256]{0:T(256)S(1)}, f32[256]{0:T(256)}, u32[]{:S(2)}) copy-start(f32[256]{0:T(256)} %get-tuple-element.328) | copy-start | bytes 3076
  304.2 5.0 collective-permute-start.1
  310.5 299.6 %copy-start.9 = (f32[32,8,256]{2,1,0:T(8,128)}, f32[32,8,256]{2,1,0:T(8,128)S(1)}, u32[]{:S(2)}) copy-start(f32[32,8,256]{2,1,0:T(8,128)S(1)} %get-tuple-element.62) | copy-start | bytes 786436
  310.5 299.6 %copy-start.11 = (f32[1,32,8,256]{3,2,1,0:T(8,128)}, f32[1,32,8,256]{3,2,1,0:T(8,128)S(1)}, u32[]{:S(2)}) copy-start(f32[1,32,8,256]{3,2,1,0:T(8,128)S(1)} %get-tuple-element.67) | copy-start | bytes 786436
  349.8 7.8 collective-permute-start.2
  512.8 67.3 %copy-start.39 = (f32[32,8,256]{2,1,0:T(8,128)}, f32[32,8,256]{2,1,0:T(8,128)S(1)}, u32[]{:S(2)}) copy-start(f32[32,8,256]{2,1,0:T(8,128)S(1)} %get-tuple-element.175) | copy-start | bytes 786436
  581.6 5.0 collective-permute-start.3
  632.3 8.5 collective-permute-start.4
  866.1 5.3 collective-permute-start.5
  923.7 8.0 collective-permute-start.7
  929.0 4.8 collective-permute-start.6
  (159 other events, 691.9 us)
where the time goes:
time: 1060 us; the launch traced here: 1040 us
  blocking collectives  741 us (70%)
  local copies, waits for them, and re-layouts  148 us (14%)
  other arithmetic  88.9 us (8%)
  waiting for transfers between devices  23.1 us (2%)
  starting transfers between devices  21.4 us (2%)
  matrix products  13.8 us (1%)
    all_gather x9, blocking collectives, line_inverse(): lax.all_gather(behind[..., 0][None], 'lon', axis=0, tiled=True)  277 us
    all_gather x9, blocking collectives, line_inverse(): lax.all_gather(ahead[..., -1][None], 'lon', axis=0, tiled=True)  276 us
    psum x8, blocking collectives, lon_total(): return lax.psum(values, 'lon')  159 us
    unnamed x355, local copies, waits for them, and re-layouts  40.6 us
  transfers between devices with their start and end apart: 10, of which 6 were waited for; matrix products, arithmetic and copies ran while one was open for 4% of the time, Pallas kernels for 0%

commit v1 on v0

v1 whole, which is shorter than its diff:
```python
import functools
import math

import jax
import jax.numpy as jnp
from jax import lax
from jax.experimental import pallas as pl
from jax.experimental.pallas import tpu as pltpu
from jax.sharding import PartitionSpec as P

KDIM = 4
SWEEPS = 3
SQUARINGS = 16
TAYLOR = 8
SOLVES = KDIM - 1
LANES = 128
ROWS = 8
MESH = pl.DeviceIdType.MESH
highest = lax.Precision.HIGHEST
epsilon = 1e-06

TILES = []
for _t in range(SOLVES):
    TILES += [_t + 1, 1, 1]
TILES += [2]
OFFSETS = [sum(TILES[:x]) for x in range(len(TILES))]
LAST = len(TILES) - 1


def kernel(n_lev, n_lon, lon_all, modes, cells, x_ref, tm_ref, fm_ref, k_ref, sh_ref, out_ref,
           g_ref, b_ref, u_ref, v_ref, p_ref, src_ref, fa_ref, fb_ref, sol_ref, wa_ref, wb_ref,
           wt_ref, tt_ref, sbuf, rbuf, lev_send, lev_recv, lon_send, lon_recv):
    chunks = LANES // modes
    n_chip = n_lev // 2
    lev = lax.axis_index("lev")
    lon = lax.axis_index("lon")
    chip, core = lev // 2, lev % 2
    partner = chip * 2 + (1 - core)

    def chip_peer(offset):
        return lax.rem(chip + offset, n_chip) * 2 + core

    barrier = pltpu.get_barrier_semaphore()
    for off in range(1, n_lon):
        pl.semaphore_signal(barrier, inc=1, device_id=(lev, lax.rem(lon + off, n_lon)), device_id_type=MESH)
    for off in range(1, n_chip):
        pl.semaphore_signal(barrier, inc=1, device_id=(chip_peer(off), lon), device_id_type=MESH)
    pl.semaphore_signal(barrier, inc=1, device_id=(partner, lon), device_id_type=MESH)
    pl.semaphore_wait(barrier, n_lon - 1 + n_chip)

    def lev_copy(turn, slot_from, slot_to, field, target, send_no):
        return pltpu.make_async_remote_copy(
            src_ref=g_ref.at[turn, slot_from, field],
            dst_ref=g_ref.at[turn, slot_to, field],
            send_sem=lev_send.at[turn, send_no, field],
            recv_sem=lev_recv.at[turn, slot_to, field],
            device_id=(target, lon),
            device_id_type=MESH,
        )

    def start_field(turn, field):
        for off in range(1, n_chip):
            lev_copy(turn, 0, 2 * off, field, chip_peer(off), off - 1).start()
        lev_copy(turn, 0, 1, field, partner, n_chip - 1).start()

    def relay_field(turn, field):
        for off in range(1, n_chip):
            lev_copy(turn, 2 * off, 2 * off, field, chip_peer(off), off - 1).wait_recv()
            lev_copy(turn, 2 * off, 2 * off + 1, field, partner, n_chip - 1 + off).start()

    def finish_field(turn, field):
        lev_copy(turn, 0, 1, field, partner, n_chip - 1).wait_recv()
        for off in range(1, n_chip):
            lev_copy(turn, 2 * off, 2 * off + 1, field, partner, n_chip - 1 + off).wait_recv()

    def mixed(turn, field):
        joined = jnp.concatenate([g_ref[turn, slot, field] for slot in range(n_lev)], axis=-1)
        return jnp.dot(joined, b_ref[turn], precision=highest, preferred_element_type=jnp.float32)

    for field in range(3):
        g_ref[0, 0, field] = x_ref[field]
        start_field(0, field)

    row = lax.broadcasted_iota(jnp.int32, (ROWS, LANES), 0)
    lane = lax.broadcasted_iota(jnp.int32, (ROWS, LANES), 1)
    group = lane // modes

    spread_row = lax.broadcasted_iota(jnp.int32, (modes, LANES), 0)
    spread_lane = lax.broadcasted_iota(jnp.int32, (modes, LANES), 1)
    repeat = jnp.where(spread_lane % modes == spread_row, 1.0, 0.0).astype(jnp.float32)
    big_row = lax.broadcasted_iota(jnp.int32, (LANES, LANES), 0) // modes
    big_lane = lax.broadcasted_iota(jnp.int32, (LANES, LANES), 1) // modes
    diagonal = big_row == big_lane
    for turn, mat_ref in enumerate((tm_ref, fm_ref)):
        mine = mat_ref[pl.ds(pl.multiple_of(lev * modes, modes), modes), :]
        tt_ref[...] = lax.dot_general(mine, repeat, (((0,), (0,)), ((), ())), precision=highest,
                                      preferred_element_type=jnp.float32)
        for off in range(n_chip):
            owner_chip = lax.rem(chip - off + n_chip, n_chip)
            for other in range(2):
                owner = owner_chip * 2 + (core if other == 0 else 1 - core)
                block = tt_ref[pl.ds(pl.multiple_of(owner * modes, modes), modes), :]
                tiled = jnp.concatenate([block] * chunks, axis=0)
                slot = 2 * off + other
                b_ref[turn, slot * LANES:(slot + 1) * LANES, :] = jnp.where(diagonal, tiled, 0.0)

    spacing = 2.0 * math.pi / lon_all

    def by_row(values):
        result = jnp.zeros((ROWS, LANES), jnp.float32)
        for number, value in enumerate(values):
            result = jnp.where(row == number, jnp.float32(value), result)
        return result

    faces = [math.sin((j + 1.0) * spacing) for j in range(ROWS - 1)] + [0.0]
    centre = by_row([math.sin((j + 0.5) * spacing) for j in range(ROWS)])
    face = by_row(faces)
    below = by_row([0.0] + faces[:-1])
    inv_centre = 1.0 / centre
    k = jnp.broadcast_to(k_ref[...], (ROWS, LANES))
    weight_p = centre / k

    def power(base, exponent):
        result, square = None, base
        while exponent:
            if exponent & 1:
                result = square if result is None else result * square
            exponent >>= 1
            if exponent:
                square = square * square
        return jnp.ones_like(base) if result is None else result

    def lane_power(base, index):
        result, square, bit = jnp.ones_like(base), base, 1
        while bit < chunks:
            result = jnp.where((index & bit) != 0, result * square, result)
            square = square * square
            bit *= 2
        return result

    class Line:
        pass

    lines = []
    for t in range(SOLVES):
        line = Line()
        g = jnp.full((ROWS, LANES), sh_ref[t], jnp.float32)
        coef = k * inv_centre * inv_centre
        half = 0.5 * (g * g + k * (face + below) * inv_centre) / coef
        q = half + jnp.sqrt(half * (half + 2.0))
        line.r = 1.0 / (1.0 + q)
        gamma = line.r / (coef * (q * line.r) * (1.0 + line.r))
        line.inv_r = 1.0 + q
        line.inv_g = 1.0 / g
        line.src_p = gamma * g
        line.src_d = gamma * k * inv_centre
        line.up = gamma * k * face * inv_centre
        line.down = gamma * k * below * inv_centre
        line.r_n = power(line.r, cells)
        line.weight_a = lane_power(line.r_n, chunks - 1 - group)
        line.weight_b = lane_power(line.r_n, group)
        r_block = power(line.r_n, chunks)
        inv_den = 1.0 / (1.0 - power(r_block, n_lon))
        block_powers = [inv_den]
        for d in range(1, n_lon):
            block_powers.append(block_powers[-1] * r_block)
        for d in range(n_lon):
            wt_ref[t, d] = jnp.where(group == 0, block_powers[d],
                                     jnp.where(group == 1, block_powers[(n_lon - 2 - d) % n_lon], 1.0))
        ones = jnp.ones((1, ROWS, LANES), jnp.float32)
        wb_ref[t, 0:1] = ones
        wa_ref[t, cells - 1:cells] = ones
        step, factor = 1, line.r
        while step < cells:
            wb_ref[t, step:2 * step] = wb_ref[t, 0:step] * factor
            wa_ref[t, cells - 2 * step:cells - step] = wa_ref[t, cells - step:cells] * factor
            factor = factor * factor
            step *= 2
        lines.append(line)

    for field, target in enumerate((u_ref, v_ref, p_ref)):
        relay_field(0, field)
        finish_field(0, field)
        target[0, 0:cells] = mixed(0, field).reshape(cells, ROWS, LANES)

    def lane_total(tile):
        step = modes
        while step < LANES:
            tile = tile + pltpu.roll(tile, step, 1)
            step *= 2
        return tile

    def spread(tile, number):
        return lane_total(jnp.where(group == number, tile, 0.0))

    def dots_tile(values):
        tile = jnp.zeros((ROWS, LANES), jnp.float32)
        for number, value in enumerate(values):
            tile = jnp.where(row == number, jnp.sum(value, axis=0, keepdims=True), tile)
        return lane_total(tile)

    def product(first, second):
        total = (centre * (u_ref[first] * u_ref[second]) + face * (v_ref[first] * v_ref[second])
                 + weight_p * (p_ref[first, 0:cells] * p_ref[second, 0:cells]))
        return jnp.sum(total, axis=0)

    def send(x, tiles):
        count, base = TILES[x], n_lon * OFFSETS[x]
        for number, tile in enumerate(tiles):
            sbuf[OFFSETS[x] + number] = tile
            rbuf[base + (n_lon - 1) * count + number] = tile
        for off in range(1, n_lon):
            pltpu.make_async_remote_copy(
                src_ref=sbuf.at[pl.ds(OFFSETS[x], count)],
                dst_ref=rbuf.at[pl.ds(base + (off - 1) * count, count)],
                send_sem=lon_send.at[x],
                recv_sem=lon_recv.at[x],
                device_id=(lev, lax.rem(lon + off, n_lon)),
                device_id_type=MESH,
            ).start()

    def whole_copy(x):
        part = rbuf.at[pl.ds(n_lon * OFFSETS[x], (n_lon - 1) * TILES[x])]
        return pltpu.make_async_remote_copy(
            src_ref=part, dst_ref=part, send_sem=lon_send.at[x], recv_sem=lon_recv.at[x],
            device_id=(lev, lax.rem(lon + 1, n_lon)), device_id_type=MESH,
        )

    def received(x, number, t=None):
        count, base = TILES[x], n_lon * OFFSETS[x]
        terms = []
        for d in range(n_lon):
            tile = rbuf[base + d * count + number]
            terms.append(tile if t is None else tile * wt_ref[t, d])
        while len(terms) > 1:
            terms = [sum(terms[i:i + 2][1:], terms[i]) for i in range(0, len(terms), 2)]
        return terms[0]

    def ends(t, slot, carry):
        line = lines[t]
        source = src_ref[slot]
        end_a = jnp.sum(wa_ref[t] * source, axis=0) + carry * line.inv_r
        end_b = jnp.sum(wb_ref[t] * source, axis=0) + carry * line.r_n
        return end_a, end_b

    def ends_tile(t, pair, dots=None):
        line = lines[t]
        total_a = lane_total(pair[0] * line.weight_a)
        total_b = lane_total(pair[1] * line.weight_b)
        rest = jnp.zeros_like(total_a) if dots is None else dots
        return jnp.where(group == 0, total_a, jnp.where(group == 1, total_b, rest))

    def local_prefix(t, pair):
        line = lines[t]
        ahead = jnp.where(group >= 1, pltpu.roll(pair[0], modes, 1), 0.0)
        behind = jnp.where(group < chunks - 1, pltpu.roll(pair[1], LANES - modes, 1), 0.0)
        step, factor = 1, line.r_n
        while step < chunks:
            ahead = ahead + jnp.where(group >= step, factor * pltpu.roll(ahead, step * modes, 1), 0.0)
            behind = behind + jnp.where(group < chunks - step,
                                        factor * pltpu.roll(behind, LANES - step * modes, 1), 0.0)
            factor = factor * factor
            step *= 2
        return ahead, behind

    def runs(t, carries):
        r = lines[t].r
        zero = jnp.zeros((ROWS, LANES), jnp.float32)

        def step(i, state):
            j = cells - 1 - i
            following = []
            for slot, (a, b) in enumerate(state):
                a = r * a + src_ref[slot, i]
                fa_ref[slot, i] = a
                b = r * b
                fb_ref[slot, j] = b
                following.append((a, b + src_ref[slot, j]))
            return tuple(following)

        lax.fori_loop(0, cells, step, tuple((zero, carry) for carry in carries), unroll=8)

    def incoming(t, x, number, local, tile=None):
        line = lines[t]
        if tile is None:
            tile = received(x, number, t)
        in_a = spread(tile, 0) * line.weight_b + local[0]
        in_b = spread(tile, 1) * line.weight_a + local[1]
        return in_a, in_b

    def first_source(t, vector, slot):
        line = lines[t]
        flux = face * v_ref[vector]
        below_flux = pltpu.roll(flux, 1, 1)
        rest = line.src_p * p_ref[vector, 0:cells] - line.src_d * (u_ref[vector] + flux - below_flux)
        src_ref[slot] = rest
        src_ref[slot, 1:cells] = src_ref[slot, 1:cells] + line.src_d * u_ref[vector, 0:cells - 1]
        return line.src_d * u_ref[vector, cells - 1]

    def coupled(t):
        line = lines[t]
        solved = sol_ref[...]
        src_ref[0] = (src_ref[3] + line.up * pltpu.roll(solved, ROWS - 1, 1)
                      + line.down * pltpu.roll(solved, 1, 1))

    def scalar(tile, number):
        return jnp.broadcast_to(tile[number:number + 1, :], (ROWS, LANES))

    norms = []
    for t in range(SOLVES):
        line = lines[t]
        x = 3 * t
        vectors = [t] + list(range(t))
        carries, pairs = [], []
        for slot, vector in enumerate(vectors):
            carries.append(first_source(t, vector, slot))
            pairs.append(ends(t, slot, carries[-1]))
        dots = dots_tile([product(i, t) for i in range(t)]) if t else None
        if t == 0:
            dots = pltpu.roll(p_ref[0, 0], (3 * modes) % LANES, 1)
        send(x, [ends_tile(t, pair, dots if n == 0 else None) for n, pair in enumerate(pairs)])
        runs(t, carries)
        locals_ = [local_prefix(t, pair) for pair in pairs]
        whole_copy(x).wait_recv()
        tile = received(x, 0, t)
        carry, pair = carries[0], pairs[0]
        inc = incoming(t, x, 0, locals_[0], tile)
        ahead, behind, source = fa_ref[0], fb_ref[0], src_ref[0]
        coefs = []
        if t == 0:
            halo = spread(rbuf[n_lon * OFFSETS[x] + (n_lon - 2) * TILES[x]], 3)
            p_ref[0, cells] = jnp.where(group == chunks - 1, halo, pltpu.roll(p_ref[0, 0], LANES - modes, 1))
        else:
            sums = spread(tile, 2)
            for i in range(t):
                c = scalar(sums, i)
                coefs.append(c)
                other = incoming(t, x, i + 1, locals_[i + 1])
                inc = (inc[0] - c * other[0], inc[1] - c * other[1])
                carry = carry - c * carries[i + 1]
                ahead = ahead - c * fa_ref[i + 1]
                behind = behind - c * fb_ref[i + 1]
                source = source - c * src_ref[i + 1]
        src_ref[3] = source
        sol_ref[...] = (ahead + behind + wb_ref[t] * (line.r * inc[0]) + wa_ref[t] * (line.r * inc[1]))
        coupled(t)
        pair = ends(t, 0, carry)
        send(x + 1, [ends_tile(t, pair)])
        runs(t, [carry])
        local = local_prefix(t, pair)
        if t:
            for ref in (u_ref, v_ref, p_ref):
                value = ref[t]
                for i in range(t):
                    value = value - coefs[i] * ref[i]
                ref[t] = value
        norm_dots = dots_tile([product(t, t)])
        whole_copy(x + 1).wait_recv()
        inc = incoming(t, x + 1, 0, local)
        sol_ref[...] = (fa_ref[0] + fb_ref[0] + wb_ref[t] * (line.r * inc[0]) + wa_ref[t] * (line.r * inc[1]))
        coupled(t)
        pair = ends(t, 0, carry)
        send(x + 2, [ends_tile(t, pair, norm_dots)])
        runs(t, [carry])
        local = local_prefix(t, pair)
        whole_copy(x + 2).wait_recv()
        tile = received(x + 2, 0, t)
        inc = incoming(t, x + 2, 0, local, tile)
        norm = jnp.sqrt(scalar(spread(tile, 2), 0) + epsilon)
        norms.append(norm)
        scale = 1.0 / norm
        for ref in (u_ref, v_ref, p_ref):
            ref[t] = ref[t] * scale
        p_ref[t + 1, 0:cells] = (fa_ref[0] + fb_ref[0] + wb_ref[t] * (line.r * inc[0])
                                 + wa_ref[t] * (line.r * inc[1])) * scale
        p_ref[t + 1, cells] = (line.r * (pair[0] + line.r_n * inc[0]) + inc[1]) * scale
        solved = p_ref[t + 1, 0:cells]
        u_ref[t + 1] = (u_ref[t] - (p_ref[t + 1, 1:cells + 1] - solved) * inv_centre) * line.inv_g
        north = jnp.where(row < ROWS - 1, 1.0, 0.0)
        v_ref[t + 1] = (v_ref[t] - (pltpu.roll(solved, ROWS - 1, 1) - solved) * north) * line.inv_g

    def half_product(first, second):
        solved = p_ref[second, 0:cells]
        east = p_ref[second, 1:cells + 1] - solved
        north = pltpu.roll(solved, ROWS - 1, 1) - solved
        return jnp.sum(u_ref[first] * east + face * (v_ref[first] * north), axis=0)

    pairs6 = [(0, 1), (0, 2), (1, 2), (0, 3), (1, 3), (2, 3)]
    skew_sums = [half_product(b, a) - half_product(a, b) for a, b in pairs6]
    grams = [product(0, 1), product(0, 2), product(1, 2), product(0, 0), product(1, 1), product(2, 2)]
    projections = [product(i, 3) for i in range(3)] + [product(3, 3)]
    values = skew_sums + grams + projections
    send(LAST, [dots_tile(values[:8]), dots_tile(values[8:])])
    whole_copy(LAST).wait_recv()
    total = [received(LAST, 0), received(LAST, 1)]
    small = [scalar(total[n // 8], n % 8) for n in range(16)]
    k01, k02, k12, k03, k13, k23 = small[0:6]
    g01, g02, g12, g00, g11, g22 = small[6:12]
    c0, c1, c2, square = small[12:16]
    norm_sq = (square - 2.0 * (c0 * c0 + c1 * c1 + c2 * c2)
               + (c0 * c0 * g00 + c1 * c1 * g11 + c2 * c2 * g22)
               + 2.0 * (c0 * c1 * g01 + c0 * c2 * g02 + c1 * c2 * g12))
    inv_last = 1.0 / jnp.sqrt(jnp.maximum(norm_sq, 0.0) + epsilon)
    a03 = (k03 - (c1 * k01 + c2 * k02)) * inv_last
    a13 = (k13 - (c2 * k12 - c0 * k01)) * inv_last
    a23 = (k23 + (c0 * k02 + c1 * k12)) * inv_last
    zero = jnp.zeros_like(k01)
    matrix = [[zero, k01, k02, a03], [-k01, zero, k12, a13], [-k02, -k12, zero, a23], [-a03, -a13, -a23, zero]]
    scaled = [[value * (1.0 / 2.0**SQUARINGS) for value in line_] for line_ in matrix]

    def times(first, second):
        return [[(first[i][0] * second[0][j] + first[i][1] * second[1][j])
                 + (first[i][2] * second[2][j] + first[i][3] * second[3][j]) for j in range(KDIM)]
                for i in range(KDIM)]

    excess = [[value * (1.0 / TAYLOR) for value in line_] for line_ in scaled]
    for degree in range(TAYLOR - 1, 0, -1):
        grown = times(scaled, excess)
        excess = [[(scaled[i][j] + grown[i][j]) * (1.0 / degree) for j in range(KDIM)] for i in range(KDIM)]

    def square_step(_, flat):
        current = [list(flat[KDIM * i:KDIM * (i + 1)]) for i in range(KDIM)]
        squared = times(current, current)
        return tuple(2.0 * current[i][j] + squared[i][j] for i in range(KDIM) for j in range(KDIM))

    flat = lax.fori_loop(0, SQUARINGS, square_step, tuple(v for line_ in excess for v in line_))
    column = [flat[KDIM * i] + (1.0 if i == 0 else 0.0) for i in range(KDIM)]
    last = norms[0] * column[3] * inv_last
    mix = [norms[0] * column[i] - last * c for i, c in enumerate((c0, c1, c2))] + [last]

    for field, ref in enumerate((u_ref, v_ref, p_ref)):
        stepped = mix[0] * ref[0, 0:cells]
        for b in range(1, KDIM):
            stepped = stepped + mix[b] * ref[b, 0:cells]
        g_ref[1, 0, field] = stepped.reshape(cells * ROWS, LANES)
        start_field(1, field)
    for field in range(3):
        relay_field(1, field)
        finish_field(1, field)
        out_ref[field] = mixed(1, field)

    for turn in range(2):
        for field in range(3):
            for off in range(1, n_chip):
                lev_copy(turn, 0, 2 * off, field, chip_peer(off), off - 1).wait_send()
                lev_copy(turn, 2 * off, 2 * off + 1, field, partner, n_chip - 1 + off).wait_send()
            lev_copy(turn, 0, 1, field, partner, n_chip - 1).wait_send()
    for x in range(len(TILES)):
        whole_copy(x).wait_send()


def body(n_lev, n_lon, wave_state, to_modes, from_modes, courant, shifts):
    fields, modes, rows, span = wave_state.shape
    chunks = LANES // modes
    cells = span // chunks
    packed = wave_state.reshape(fields, modes, rows, chunks, cells)
    packed = packed.transpose(0, 4, 2, 3, 1).reshape(fields, cells * rows, LANES)
    speeds = jnp.tile(courant, chunks)[None, :]
    total = sum(TILES)
    block = (cells, ROWS, LANES)
    f32 = jnp.float32
    vmem = pl.BlockSpec(memory_space=pltpu.VMEM)
    result = pl.pallas_call(
        functools.partial(kernel, n_lev, n_lon, span * n_lon, modes, cells),
        out_shape=jax.ShapeDtypeStruct(packed.shape, f32),
        in_specs=[vmem, vmem, vmem, vmem, pl.BlockSpec(memory_space=pltpu.SMEM)],
        out_specs=vmem,
        scratch_shapes=[
            pltpu.VMEM((2, n_lev, fields, cells * rows, LANES), f32),
            pltpu.VMEM((2, n_lev * LANES, LANES), f32),
            pltpu.VMEM((KDIM,) + block, f32),
            pltpu.VMEM((KDIM,) + block, f32),
            pltpu.VMEM((KDIM, cells + 1, ROWS, LANES), f32),
            pltpu.VMEM((4,) + block, f32),
            pltpu.VMEM((3,) + block, f32),
            pltpu.VMEM((3,) + block, f32),
            pltpu.VMEM(block, f32),
            pltpu.VMEM((SOLVES,) + block, f32),
            pltpu.VMEM((SOLVES,) + block, f32),
            pltpu.VMEM((SOLVES, n_lon, ROWS, LANES), f32),
            pltpu.VMEM((n_lev * modes, LANES), f32),
            pltpu.VMEM((total, ROWS, LANES), f32),
            pltpu.VMEM((n_lon * total, ROWS, LANES), f32),
            pltpu.SemaphoreType.DMA((2, n_lev - 1, 3)),
            pltpu.SemaphoreType.DMA((2, n_lev, 3)),
            pltpu.SemaphoreType.DMA((len(TILES),)),
            pltpu.SemaphoreType.DMA((len(TILES),)),
        ],
        compiler_params=pltpu.CompilerParams(
            collective_id=0, has_side_effects=True, vmem_limit_bytes=40 * 1024 * 1024),
        name="krylov",
    )(packed, to_modes, from_modes, speeds, shifts)
    result = result.reshape(fields, cells, rows, chunks, modes).transpose(0, 4, 2, 3, 1)
    return result.reshape(fields, modes, rows, span)


def solution(mesh):
    n_lev, n_lon = mesh.shape["lev"], mesh.shape["lon"]
    in_specs = (P(None, "lev", None, "lon"), P(), P(), P("lev"), P())
    out_specs = P(None, "lev", None, "lon")
    return jax.shard_map(functools.partial(body, n_lev, n_lon), mesh=mesh, in_specs=in_specs,
                         out_specs=out_specs, check_vma=False)
```

time: 1060 us -> 110 us (0.10); the launches traced: 1040 us -> 110 us
  blocking collectives: 741 us -> 0 us
  local copies, waits for them, and re-layouts: 148 us -> 17.3 us
  Pallas kernels: 0 us -> 92.4 us
  other arithmetic: 88.9 us -> 0 us
  waiting for transfers between devices: 23.1 us -> 0 us
  starting transfers between devices: 21.4 us -> 0 us
  matrix products: 13.8 us -> 0 us
    all_gather x18 -> x0, blocking collectives: 553 us -> none  [the longest x9 277 us: line_inverse(): lax.all_gather(behind[..., 0][None], 'lon', axis=0, tiled=True)]
    psum x8 -> x0, blocking collectives: 159 us -> none  [lon_total(): return lax.psum(values, 'lon')]
    pallas_call x0 -> x1, Pallas kernels: none -> 92.4 us  [body(): pl.pallas_call(functools.partial(kernel, n_lev, n_lon, span * n_lon, mode...]
    slice x151 -> x0, local copies, waits for them, and re-layouts: 43.5 us -> none  [the longest x18 10.5 us: line_inverse(): behind[..., 0][None]]
    unnamed x355 -> x8, local copies, waits for them, and re-layouts: 40.6 us -> 0.01 us
    all_to_all x2 -> x0, blocking collectives: 29 us -> none  [the longest x1 14.6 us: regroup(): lax.all_to_all(fields, 'lev', split_axis=3, concat_axis=1, tiled=True)]
    add x83 -> x0, other arithmetic: 23.5 us -> none  [the longest x72 15.1 us: geometric_run(): result = result + factor * shifted]
    reduce_sum x22 -> x0, other arithmetic: 20.6 us -> none  [the longest x13 13.5 us: inner_product(): return jnp.sum(weighted, axis=(-2, -1))]
  transfers between devices with their start and end apart: 10 -> 0, of which waited for: 6 -> 0; matrix products, arithmetic and copies ran while one was open for 4% -> 0% of each run, Pallas kernels for 0% -> 0%
where the time goes in v1:
time: 110 us
  Pallas kernels  92.4 us (84%)
  local copies, waits for them, and re-layouts  17.3 us (16%)
    pallas_call x1, Pallas kernels, body(): pl.pallas_call(functools.partial(kernel, n_lev, n_lon, span * n_lon, mode...  92.4 us
    reshape x2, local copies, waits for them, and re-layouts, body(): packed = wave_state.reshape(fields, modes, rows, chunks, cells)  5.54 us
    transpose x1, local copies, waits for them, and re-layouts, body(): result.reshape(fields, cells, rows, chunks, modes).transpose(0, 4, 2, 3, 1)  4.03 us
    reshape x1, local copies, waits for them, and re-layouts, body(): result.reshape(fields, cells, rows, chunks, modes).transpose(0, 4, 2, 3, 1)  2.95 us
    reshape x1, local copies, waits for them, and re-layouts, body(): packed.transpose(0, 4, 2, 3, 1).reshape(fields, cells * rows, LANES)  2.87 us

profile of v1, /device:TPU:0, one launch (start us, length us, event | category | flops | bytes accessed | tf_op | source)
XLA Modules:
  0.0 109.7 jit_solution(10446729487996016191)
XLA Ops:
  0.0 1.9 %reshape.13 = f32[3,32,8,4,64]{4,3,2,1,0:T(4,128)S(1)} reshape(f32[3,32,8,256]{3,2,1,0:T(8,128)} %param.5) | data formatting | bytes 1572864 | tf_op jit(solution)/shard_map/reshape | solution.py:456
  1.9 3.7 %copy.9 = f32[3,32,8,4,64]{1,3,2,4,0:T(4,128)} copy(f32[3,32,8,4,64]{4,3,2,1,0:T(4,128)S(1)} %reshape.13) | data formatting | bytes 1572864 | tf_op jit(solution)/shard_map/reshape | solution.py:456
  5.6 0.0 copy-start.3
  5.6 0.0 copy-start
  5.6 0.0 copy-start.1
  5.6 0.0 copy-start.2
  5.6 2.9 %reshape.14.x_ref = f32[3,512,128]{2,1,0:T(8,128)S(1)} reshape(f32[3,64,8,4,32]{4,3,2,1,0:T(4,128)} %bitcast.4) | data formatting | bytes 1572864 | tf_op jit(solution)/shard_map/reshape | solution.py:457
  8.4 0.0 copy-done.3
  8.5 0.1 broadcast_in_dim_tile.3.k_ref
  8.5 0.0 copy-done
  8.6 0.0 copy-done.1
  8.6 0.0 copy-done.2
  8.6 92.4 %krylov.1 = f32[3,512,128]{2,1,0:T(8,128)S(1)} custom-call(f32[3,512,128]{2,1,0:T(8,128)S(1)} %reshape.14.x_ref, f32[128,128]{1,0:T(8,128)S(1)} %copy-done, f32[128,128]{1,0:T(8,128)S(1)} %copy-done.1, f32[1,128]{1,0:T(1,128)S(1)} %broadcast_in_dim_tile.3.k_ref, f32[3]{0:T(128)S(1)} %copy-done.2), custom_call_target="tpu_custom_call" | custom-call | tf_op jit(solution)/shard_map/krylov/pallas_call | solution.py:463
  100.9 3.0 %reshape.15 = f32[3,64,8,4,32]{4,3,2,1,0:T(4,128)} reshape(f32[3,512,128]{2,1,0:T(8,128)S(1)} %krylov.1) | data formatting | bytes 1572864 | tf_op jit(solution)/shard_map/reshape | solution.py:493
  103.9 4.0 %copy.10 = f32[3,32,8,4,64]{4,3,2,1,0:T(4,128)S(1)} copy(f32[3,32,8,4,64]{1,3,2,4,0:T(4,128)} %bitcast.5) | data formatting | bytes 1572864 | tf_op jit(solution)/shard_map/transpose | solution.py:493
  107.9 1.8 %reshape.16 = f32[3,32,8,256]{3,2,1,0:T(8,128)} reshape(f32[3,32,8,4,64]{4,3,2,1,0:T(4,128)S(1)} %copy.10) | data formatting | bytes 1572864 | tf_op jit(solution)/shard_map/reshape | solution.py:494
  (1 shorter events, 0.0 us)
Async XLA Ops:
  5.6 2.9 %copy-start.3 = (f32[32]{0:T(128)S(1)}, f32[32]{0:T(128)}, u32[]{:S(2)}) copy-start(f32[32]{0:T(128)} %param.8) | copy-start | bytes 388
  5.6 3.0 %copy-start = (f32[128,128]{1,0:T(8,128)S(1)}, f32[128,128]{1,0:T(8,128)}, u32[]{:S(2)}) copy-start(f32[128,128]{1,0:T(8,128)} %tm_ref.1) | copy-start | bytes 196612
  5.6 3.0 %copy-start.1 = (f32[128,128]{1,0:T(8,128)S(1)}, f32[128,128]{1,0:T(8,128)}, u32[]{:S(2)}) copy-start(f32[128,128]{1,0:T(8,128)} %fm_ref.1) | copy-start | bytes 196612
  5.6 3.0 %copy-start.2 = (f32[3]{0:T(128)S(1)}, f32[3]{0:T(128)}, u32[]{:S(2)}) copy-start(f32[3]{0:T(128)} %sh_ref.1) | copy-start | bytes 40

commit v2 on v1

--- a/solution.py
+++ b/solution.py
@@ -21,15 +21,15 @@
 
 TILES = []
 for _t in range(SOLVES):
-    TILES += [_t + 1, 1, 1]
-TILES += [2]
+    TILES += [1, 1, 1, _t + 1 if _t + 1 < SOLVES else 1]
+TILES += [1]
 OFFSETS = [sum(TILES[:x]) for x in range(len(TILES))]
 LAST = len(TILES) - 1
 
 
-def kernel(n_lev, n_lon, lon_all, modes, cells, x_ref, tm_ref, fm_ref, k_ref, sh_ref, out_ref,
-           g_ref, b_ref, u_ref, v_ref, p_ref, src_ref, fa_ref, fb_ref, sol_ref, wa_ref, wb_ref,
-           wt_ref, tt_ref, sbuf, rbuf, lev_send, lev_recv, lon_send, lon_recv):
+def kernel(n_lev, n_lon, lon_all, modes, cells, halves, x_ref, tm_ref, fm_ref, k_ref, sh_ref, out_ref,
+           g_ref, h_ref, coef_ref, b_ref, u_ref, v_ref, p_ref, src_ref, fa_ref, fb_ref, sol_ref, wa_ref, wb_ref,
+           wt_ref, tt_ref, o_ref, sbuf, rbuf, lev_send, lev_recv, h_send, h_recv, coef_send, coef_recv, lon_send, lon_recv):
     chunks = LANES // modes
     n_chip = n_lev // 2
     lev = lax.axis_index("lev")
@@ -43,10 +43,9 @@
     barrier = pltpu.get_barrier_semaphore()
     for off in range(1, n_lon):
         pl.semaphore_signal(barrier, inc=1, device_id=(lev, lax.rem(lon + off, n_lon)), device_id_type=MESH)
-    for off in range(1, n_chip):
-        pl.semaphore_signal(barrier, inc=1, device_id=(chip_peer(off), lon), device_id_type=MESH)
-    pl.semaphore_signal(barrier, inc=1, device_id=(partner, lon), device_id_type=MESH)
-    pl.semaphore_wait(barrier, n_lon - 1 + n_chip)
+    for off in range(1, n_lev):
+        pl.semaphore_signal(barrier, inc=1, device_id=(lax.rem(lev + off, n_lev), lon), device_id_type=MESH)
+    pl.semaphore_wait(barrier, n_lon + n_lev - 2)
 
     def lev_copy(turn, slot_from, slot_to, field, target, send_no):
         return pltpu.make_async_remote_copy(
@@ -73,17 +72,90 @@
         for off in range(1, n_chip):
             lev_copy(turn, 2 * off, 2 * off + 1, field, partner, n_chip - 1 + off).wait_recv()
 
-    def mixed(turn, field):
-        joined = jnp.concatenate([g_ref[turn, slot, field] for slot in range(n_lev)], axis=-1)
+    def sent_fields(turn):
+        for field in range(3):
+            for off in range(1, n_chip):
+                lev_copy(turn, 0, 2 * off, field, chip_peer(off), off - 1).wait_send()
+                lev_copy(turn, 2 * off, 2 * off + 1, field, partner, n_chip - 1 + off).wait_send()
+            lev_copy(turn, 0, 1, field, partner, n_chip - 1).wait_send()
+
+    def p_copy(t, slot_from, slot_to, target, send_no):
+        return pltpu.make_async_remote_copy(
+            src_ref=h_ref.at[t, slot_from],
+            dst_ref=h_ref.at[t, slot_to],
+            send_sem=h_send.at[t, send_no],
+            recv_sem=h_recv.at[t, slot_to],
+            device_id=(target, lon),
+            device_id_type=MESH,
+        )
+
+    def start_p(t):
+        for off in range(1, n_chip):
+            p_copy(t, 0, 2 * off, chip_peer(off), off - 1).start()
+        p_copy(t, 0, 1, partner, n_chip - 1).start()
+
+    def relay_p(t):
+        for off in range(1, n_chip):
+            p_copy(t, 2 * off, 2 * off, chip_peer(off), off - 1).wait_recv()
+            p_copy(t, 2 * off, 2 * off + 1, partner, n_chip - 1 + off).start()
+
+    def finish_p(t):
+        p_copy(t, 0, 1, partner, n_chip - 1).wait_recv()
+        for off in range(1, n_chip):
+            p_copy(t, 2 * off, 2 * off + 1, partner, n_chip - 1 + off).wait_recv()
+
+    def coef_whole():
+        part = coef_ref.at[pl.ds(1, n_lev - 1)]
+        return pltpu.make_async_remote_copy(
+            src_ref=part, dst_ref=part, send_sem=coef_send.at[0], recv_sem=coef_recv.at[0],
+            device_id=(partner, lon), device_id_type=MESH,
+        )
+
+    def mixed(turn, blocks):
+        joined = jnp.concatenate(blocks, axis=-1)
         return jnp.dot(joined, b_ref[turn], precision=highest, preferred_element_type=jnp.float32)
-
-    for field in range(3):
-        g_ref[0, 0, field] = x_ref[field]
-        start_field(0, field)
 
     row = lax.broadcasted_iota(jnp.int32, (ROWS, LANES), 0)
     lane = lax.broadcasted_iota(jnp.int32, (ROWS, LANES), 1)
     group = lane // modes
+    together = LANES // cells
+    tall_group = lax.broadcasted_iota(jnp.int32, (cells, LANES), 1) // modes % together
+
+    def turned(tile, steps):
+        steps = steps * modes % LANES
+        return pltpu.roll(tile, steps, 1) if steps else tile
+
+    def chosen(tiles):
+        result = tiles[0]
+        for number in range(1, together):
+            result = jnp.where(tall_group == number, tiles[number], result)
+        return result
+
+    def pack(field):
+        for first in range(0, ROWS, together):
+            stack = jnp.concatenate(
+                [x_ref[field, :, first + n, half * LANES:(half + 1) * LANES]
+                 for half in range(halves) for n in range(together)], axis=0)
+            flipped = stack.T
+            parts = [flipped[c * cells:(c + 1) * cells] for c in range(together)]
+            for n in range(together):
+                g_ref[0, 0, field, pl.ds(first + n, cells, stride=ROWS), :] = chosen(
+                    [turned(parts[c], c - n) for c in range(together)])
+
+    def unpack(field):
+        for first in range(0, ROWS, together):
+            rows = [o_ref[pl.ds(first + n, cells, stride=ROWS), :] for n in range(together)]
+            flipped = jnp.concatenate(
+                [chosen([turned(rows[n], n - c) for n in range(together)]) for c in range(together)], axis=0)
+            stack = flipped.T
+            for half in range(halves):
+                for n in range(together):
+                    at = (half * together + n) * modes
+                    out_ref[field, :, first + n, half * LANES:(half + 1) * LANES] = stack[at:at + modes]
+
+    for field in range(3):
+        pack(field)
+        start_field(0, field)
 
     spread_row = lax.broadcasted_iota(jnp.int32, (modes, LANES), 0)
     spread_lane = lax.broadcasted_iota(jnp.int32, (modes, LANES), 1)
@@ -181,7 +253,10 @@
     for field, target in enumerate((u_ref, v_ref, p_ref)):
         relay_field(0, field)
         finish_field(0, field)
-        target[0, 0:cells] = mixed(0, field).reshape(cells, ROWS, LANES)
+        modal = mixed(0, [g_ref[0, slot, field] for slot in range(n_lev)])
+        target[0, 0:cells] = modal.reshape(cells, ROWS, LANES)
+        g_ref[1, 0, field] = modal
+        start_field(1, field)
 
     def lane_total(tile):
         step = modes
@@ -263,14 +338,14 @@
             step *= 2
         return ahead, behind
 
-    def runs(t, carries):
+    def runs(t, carries, slots):
         r = lines[t].r
         zero = jnp.zeros((ROWS, LANES), jnp.float32)
 
         def step(i, state):
             j = cells - 1 - i
             following = []
-            for slot, (a, b) in enumerate(state):
+            for slot, (a, b) in zip(slots, state):
                 a = r * a + src_ref[slot, i]
                 fa_ref[slot, i] = a
                 b = r * b
@@ -306,25 +381,39 @@
     def scalar(tile, number):
         return jnp.broadcast_to(tile[number:number + 1, :], (ROWS, LANES))
 
+    def half_product(first, second):
+        solved = p_ref[second, 0:cells]
+        east = p_ref[second, 1:cells + 1] - solved
+        north = pltpu.roll(solved, ROWS - 1, 1) - solved
+        return jnp.sum(u_ref[first] * east + face * (v_ref[first] * north), axis=0)
+
+    def skew_sum(a, b):
+        return half_product(b, a) - half_product(a, b)
+
     norms = []
+    earlier = []
+    scale = None
+    none = jnp.zeros((ROWS, LANES), jnp.float32)
+    wind_rows, height_rows = [], []
+    wind = height = [none + 1.0, none, none, none]
     for t in range(SOLVES):
         line = lines[t]
-        x = 3 * t
-        vectors = [t] + list(range(t))
-        carries, pairs = [], []
-        for slot, vector in enumerate(vectors):
-            carries.append(first_source(t, vector, slot))
-            pairs.append(ends(t, slot, carries[-1]))
-        dots = dots_tile([product(i, t) for i in range(t)]) if t else None
-        if t == 0:
+        x = 4 * t
+        carry = first_source(t, t, 0)
+        pair = ends(t, 0, carry)
+        if t:
+            dots = dots_tile([product(i, t) for i in range(t)])
+        else:
             dots = pltpu.roll(p_ref[0, 0], (3 * modes) % LANES, 1)
-        send(x, [ends_tile(t, pair, dots if n == 0 else None) for n, pair in enumerate(pairs)])
-        runs(t, carries)
-        locals_ = [local_prefix(t, pair) for pair in pairs]
+        send(x, [ends_tile(t, pair, dots)])
+        runs(t, [carry], [0])
+        local = local_prefix(t, pair)
+        if t:
+            whole_copy(x - 1).wait_recv()
+            others = [incoming(t, x - 1, i, earlier[i][1]) for i in range(t)]
         whole_copy(x).wait_recv()
         tile = received(x, 0, t)
-        carry, pair = carries[0], pairs[0]
-        inc = incoming(t, x, 0, locals_[0], tile)
+        inc = incoming(t, x, 0, local, tile)
         ahead, behind, source = fa_ref[0], fb_ref[0], src_ref[0]
         coefs = []
         if t == 0:
@@ -335,18 +424,18 @@
             for i in range(t):
                 c = scalar(sums, i)
                 coefs.append(c)
-                other = incoming(t, x, i + 1, locals_[i + 1])
-                inc = (inc[0] - c * other[0], inc[1] - c * other[1])
-                carry = carry - c * carries[i + 1]
-                ahead = ahead - c * fa_ref[i + 1]
-                behind = behind - c * fb_ref[i + 1]
-                source = source - c * src_ref[i + 1]
+                d = c * scale if i == t - 1 else c
+                inc = (inc[0] - d * others[i][0], inc[1] - d * others[i][1])
+                carry = carry - d * earlier[i][0]
+                ahead = ahead - d * fa_ref[i + 1]
+                behind = behind - d * fb_ref[i + 1]
+                source = source - d * src_ref[i + 1]
         src_ref[3] = source
         sol_ref[...] = (ahead + behind + wb_ref[t] * (line.r * inc[0]) + wa_ref[t] * (line.r * inc[1]))
         coupled(t)
         pair = ends(t, 0, carry)
         send(x + 1, [ends_tile(t, pair)])
-        runs(t, [carry])
+        runs(t, [carry], [0])
         local = local_prefix(t, pair)
         if t:
             for ref in (u_ref, v_ref, p_ref):
@@ -355,48 +444,63 @@
                     value = value - coefs[i] * ref[i]
                 ref[t] = value
         norm_dots = dots_tile([product(t, t)])
+        if t == 1:
+            for field in range(3):
+                relay_field(1, field)
         whole_copy(x + 1).wait_recv()
         inc = incoming(t, x + 1, 0, local)
         sol_ref[...] = (fa_ref[0] + fb_ref[0] + wb_ref[t] * (line.r * inc[0]) + wa_ref[t] * (line.r * inc[1]))
         coupled(t)
         pair = ends(t, 0, carry)
         send(x + 2, [ends_tile(t, pair, norm_dots)])
-        runs(t, [carry])
+        runs(t, [carry], [0])
         local = local_prefix(t, pair)
+        if t + 1 < SOLVES:
+            carries = [first_source(t + 1, i, i + 1) for i in range(t + 1)]
+            pairs = [ends(t + 1, i + 1, carries[i]) for i in range(t + 1)]
+            send(x + 3, [ends_tile(t + 1, other) for other in pairs])
+            runs(t + 1, carries, [i + 1 for i in range(t + 1)])
+            earlier = [(carries[i], local_prefix(t + 1, pairs[i])) for i in range(t + 1)]
+        else:
+            send(x + 3, [dots_tile([skew_sum(0, 1), skew_sum(0, 2), skew_sum(1, 2), product(0, 1),
+                                    product(0, 2), product(1, 2), product(1, 1), product(2, 2)])])
+        if t:
+            relay_p(t - 1)
         whole_copy(x + 2).wait_recv()
         tile = received(x + 2, 0, t)
         inc = incoming(t, x + 2, 0, local, tile)
         norm = jnp.sqrt(scalar(spread(tile, 2), 0) + epsilon)
         norms.append(norm)
         scale = 1.0 / norm
+        for i in range(t):
+            wind = [w - coefs[i] * e for w, e in zip(wind, wind_rows[i])]
+            height = [w - coefs[i] * e for w, e in zip(height, height_rows[i])]
+        wind_rows.append([w * scale for w in wind])
+        height_rows.append([w * scale for w in height])
+        wind = [(w + (1.0 if n == t + 1 else 0.0)) * line.inv_g for n, w in enumerate(wind_rows[t])]
+        height = [none + (1.0 if n == t + 1 else 0.0) for n in range(KDIM)]
         for ref in (u_ref, v_ref, p_ref):
             ref[t] = ref[t] * scale
         p_ref[t + 1, 0:cells] = (fa_ref[0] + fb_ref[0] + wb_ref[t] * (line.r * inc[0])
                                  + wa_ref[t] * (line.r * inc[1])) * scale
         p_ref[t + 1, cells] = (line.r * (pair[0] + line.r_n * inc[0]) + inc[1]) * scale
+        h_ref[t, 0] = p_ref[t + 1].reshape((cells + 1) * ROWS, LANES)
+        start_p(t)
         solved = p_ref[t + 1, 0:cells]
         u_ref[t + 1] = (u_ref[t] - (p_ref[t + 1, 1:cells + 1] - solved) * inv_centre) * line.inv_g
         north = jnp.where(row < ROWS - 1, 1.0, 0.0)
         v_ref[t + 1] = (v_ref[t] - (pltpu.roll(solved, ROWS - 1, 1) - solved) * north) * line.inv_g
 
-    def half_product(first, second):
-        solved = p_ref[second, 0:cells]
-        east = p_ref[second, 1:cells + 1] - solved
-        north = pltpu.roll(solved, ROWS - 1, 1) - solved
-        return jnp.sum(u_ref[first] * east + face * (v_ref[first] * north), axis=0)
-
-    pairs6 = [(0, 1), (0, 2), (1, 2), (0, 3), (1, 3), (2, 3)]
-    skew_sums = [half_product(b, a) - half_product(a, b) for a, b in pairs6]
-    grams = [product(0, 1), product(0, 2), product(1, 2), product(0, 0), product(1, 1), product(2, 2)]
-    projections = [product(i, 3) for i in range(3)] + [product(3, 3)]
-    values = skew_sums + grams + projections
-    send(LAST, [dots_tile(values[:8]), dots_tile(values[8:])])
+    values = [skew_sum(i, 3) for i in range(3)] + [product(i, 3) for i in range(3)]
+    values += [product(3, 3), product(0, 0)]
+    send(LAST, [dots_tile(values)])
+    whole_copy(LAST - 1).wait_recv()
+    total = received(LAST - 1, 0)
+    k01, k02, k12, g01, g02, g12, g11, g22 = [scalar(total, n) for n in range(ROWS)]
+    k02, k12, g02, g12, g22 = k02 * scale, k12 * scale, g02 * scale, g12 * scale, g22 * scale * scale
     whole_copy(LAST).wait_recv()
-    total = [received(LAST, 0), received(LAST, 1)]
-    small = [scalar(total[n // 8], n % 8) for n in range(16)]
-    k01, k02, k12, k03, k13, k23 = small[0:6]
-    g01, g02, g12, g00, g11, g22 = small[6:12]
-    c0, c1, c2, square = small[12:16]
+    total = received(LAST, 0)
+    k03, k13, k23, c0, c1, c2, square, g00 = [scalar(total, n) for n in range(ROWS)]
     norm_sq = (square - 2.0 * (c0 * c0 + c1 * c1 + c2 * c2)
                + (c0 * c0 * g00 + c1 * c1 * g11 + c2 * c2 * g22)
                + 2.0 * (c0 * c1 * g01 + c0 * c2 * g02 + c1 * c2 * g12))
@@ -427,24 +531,57 @@
     column = [flat[KDIM * i] + (1.0 if i == 0 else 0.0) for i in range(KDIM)]
     last = norms[0] * column[3] * inv_last
     mix = [norms[0] * column[i] - last * c for i, c in enumerate((c0, c1, c2))] + [last]
-
-    for field, ref in enumerate((u_ref, v_ref, p_ref)):
-        stepped = mix[0] * ref[0, 0:cells]
-        for b in range(1, KDIM):
-            stepped = stepped + mix[b] * ref[b, 0:cells]
-        g_ref[1, 0, field] = stepped.reshape(cells * ROWS, LANES)
-        start_field(1, field)
+    wind_rows.append(wind)
+    height_rows.append(height)
+    coefs = none
+    for n in range(KDIM):
+        wind_sum = sum([mix[b] * wind_rows[b][n] for b in range(1, KDIM)], mix[0] * wind_rows[0][n])
+        height_sum = sum([mix[b] * height_rows[b][n] for b in range(1, KDIM)], mix[0] * height_rows[0][n])
+        coefs = jnp.where(row == n, wind_sum, jnp.where(row == KDIM + n, height_sum, coefs))
+
+    coef_ref[0] = coefs
+    for off in range(n_chip):
+        for other in range(2):
+            if off or other:
+                target = lax.rem(chip + off, n_chip) * 2 + (core if other == 0 else 1 - core)
+                pltpu.make_async_remote_copy(
+                    src_ref=coef_ref.at[0], dst_ref=coef_ref.at[2 * off + other],
+                    send_sem=coef_send.at[0], recv_sem=coef_recv.at[0],
+                    device_id=(target, lon), device_id_type=MESH,
+                ).start()
+    relay_p(SOLVES - 1)
+    sent_fields(0)
     for field in range(3):
-        relay_field(1, field)
         finish_field(1, field)
-        out_ref[field] = mixed(1, field)
-
-    for turn in range(2):
+    for t in range(SOLVES):
+        finish_p(t)
+    coef_whole().wait_recv()
+    blocks = [[], [], []]
+    north = jnp.where(row < ROWS - 1, 1.0, 0.0)
+    for slot in range(n_lev):
+        weights = coef_ref[slot]
+        first = [g_ref[1, slot, field].reshape(cells, ROWS, LANES) for field in range(3)]
+        heights = [h_ref[t, slot].reshape(cells + 1, ROWS, LANES) for t in range(SOLVES)]
+        joint = sum([scalar(weights, t + 1) * heights[t] for t in range(1, SOLVES)], scalar(weights, 1) * heights[0])
+        keep = scalar(weights, 0)
+        here = joint[0:cells]
+        stepped = [keep * first[0] - inv_centre * (joint[1:cells + 1] - here),
+                   keep * first[1] - north * (pltpu.roll(here, ROWS - 1, 1) - here),
+                   sum([scalar(weights, KDIM + t + 1) * heights[t][0:cells] for t in range(SOLVES)],
+                       scalar(weights, KDIM) * first[2])]
         for field in range(3):
-            for off in range(1, n_chip):
-                lev_copy(turn, 0, 2 * off, field, chip_peer(off), off - 1).wait_send()
-                lev_copy(turn, 2 * off, 2 * off + 1, field, partner, n_chip - 1 + off).wait_send()
-            lev_copy(turn, 0, 1, field, partner, n_chip - 1).wait_send()
+            g_ref[0, slot, field] = stepped[field].reshape(cells * ROWS, LANES)
+    for field in range(3):
+        o_ref[...] = mixed(1, [g_ref[0, slot, field] for slot in range(n_lev)])
+        unpack(field)
+
+    for t in range(SOLVES):
+        for off in range(1, n_chip):
+            p_copy(t, 0, 2 * off, chip_peer(off), off - 1).wait_send()
+            p_copy(t, 2 * off, 2 * off + 1, partner, n_chip - 1 + off).wait_send()
+        p_copy(t, 0, 1, partner, n_chip - 1).wait_send()
+    coef_whole().wait_send()
+    sent_fields(1)
     for x in range(len(TILES)):
         whole_copy(x).wait_send()
 
@@ -453,20 +590,20 @@
     fields, modes, rows, span = wave_state.shape
     chunks = LANES // modes
     cells = span // chunks
-    packed = wave_state.reshape(fields, modes, rows, chunks, cells)
-    packed = packed.transpose(0, 4, 2, 3, 1).reshape(fields, cells * rows, LANES)
     speeds = jnp.tile(courant, chunks)[None, :]
     total = sum(TILES)
     block = (cells, ROWS, LANES)
     f32 = jnp.float32
     vmem = pl.BlockSpec(memory_space=pltpu.VMEM)
-    result = pl.pallas_call(
-        functools.partial(kernel, n_lev, n_lon, span * n_lon, modes, cells),
-        out_shape=jax.ShapeDtypeStruct(packed.shape, f32),
+    return pl.pallas_call(
+        functools.partial(kernel, n_lev, n_lon, span * n_lon, modes, cells, span // LANES),
+        out_shape=jax.ShapeDtypeStruct(wave_state.shape, f32),
         in_specs=[vmem, vmem, vmem, vmem, pl.BlockSpec(memory_space=pltpu.SMEM)],
         out_specs=vmem,
         scratch_shapes=[
             pltpu.VMEM((2, n_lev, fields, cells * rows, LANES), f32),
+            pltpu.VMEM((SOLVES, n_lev, (cells + 1) * rows, LANES), f32),
+            pltpu.VMEM((n_lev, ROWS, LANES), f32),
             pltpu.VMEM((2, n_lev * LANES, LANES), f32),
             pltpu.VMEM((KDIM,) + block, f32),
             pltpu.VMEM((KDIM,) + block, f32),
@@ -479,19 +616,22 @@
             pltpu.VMEM((SOLVES,) + block, f32),
             pltpu.VMEM((SOLVES, n_lon, ROWS, LANES), f32),
             pltpu.VMEM((n_lev * modes, LANES), f32),
+            pltpu.VMEM((cells * rows, LANES), f32),
             pltpu.VMEM((total, ROWS, LANES), f32),
             pltpu.VMEM((n_lon * total, ROWS, LANES), f32),
             pltpu.SemaphoreType.DMA((2, n_lev - 1, 3)),
             pltpu.SemaphoreType.DMA((2, n_lev, 3)),
+            pltpu.SemaphoreType.DMA((SOLVES, n_lev - 1)),
+            pltpu.SemaphoreType.DMA((SOLVES, n_lev)),
+            pltpu.SemaphoreType.DMA((1,)),
+            pltpu.SemaphoreType.DMA((1,)),
             pltpu.SemaphoreType.DMA((len(TILES),)),
             pltpu.SemaphoreType.DMA((len(TILES),)),
         ],
         compiler_params=pltpu.CompilerParams(
             collective_id=0, has_side_effects=True, vmem_limit_bytes=40 * 1024 * 1024),
         name="krylov",
-    )(packed, to_modes, from_modes, speeds, shifts)
-    result = result.reshape(fields, cells, rows, chunks, modes).transpose(0, 4, 2, 3, 1)
-    return result.reshape(fields, modes, rows, span)
+    )(wave_state, to_modes, from_modes, speeds, shifts)
 
 
 def solution(mesh):

time: 110 us -> 90.3 us (0.82)
  local copies, waits for them, and re-layouts: 17.3 us -> 5 us
  Pallas kernels: 92.4 us -> 85.1 us
    reshape x5 -> x0, local copies, waits for them, and re-layouts: 13.1 us -> none  [the longest x2 5.54 us: body(): packed = wave_state.reshape(fields, modes, rows, chunks, cells)]
    pallas_call x1, Pallas kernels: 92.4 us -> 85.1 us  [body(): pl.pallas_call(functools.partial(kernel, n_lev, n_lon, span * n_lon, mode...]
    unnamed x8 -> x9, local copies, waits for them, and re-layouts: 0.01 us -> 4.26 us
    transpose x1 -> x0, local copies, waits for them, and re-layouts: 4.03 us -> none  [body(): result.reshape(fields, cells, rows, chunks, modes).transpose(0, 4, 2, 3, 1)]
where the time goes in v2:
time: 90.3 us; the launch traced here: 90.1 us
  Pallas kernels  85.1 us (94%)
  local copies, waits for them, and re-layouts  5 us (6%)
    pallas_call x1, Pallas kernels, body(): pl.pallas_call(functools.partial(kernel, n_lev, n_lon, span * n_lon, mode...  85.1 us
    unnamed x9, local copies, waits for them, and re-layouts  4.26 us

profile of v2, /device:TPU:0, one launch (start us, length us, event | category | flops | bytes accessed | tf_op | source)
XLA Modules:
  0.0 90.1 jit_solution(3760391162663139011)
XLA Ops:
  0.0 0.7 tile.2
  0.7 0.0 copy-start.3
  0.7 0.1 broadcast_in_dim_tile.3.k_ref
  0.7 0.6 copy-done.3
  1.3 0.0 copy-start
  1.3 1.1 %copy-done = f32[3,32,8,256]{3,2,1,0:T(8,128)S(1)} copy-done((f32[3,32,8,256]{3,2,1,0:T(8,128)S(1)}, f32[3,32,8,256]{3,2,1,0:T(8,128)}, u32[]{:S(2)}) %copy-start) | copy-done | bytes 786456
  2.4 0.0 copy-start.1
  2.4 0.8 copy-done.1
  3.3 0.0 copy-start.2
  3.3 0.8 copy-done.2
  4.1 85.1 %krylov.1 = f32[3,32,8,256]{3,2,1,0:T(8,128)S(1)} custom-call(f32[3,32,8,256]{3,2,1,0:T(8,128)S(1)} %copy-done, f32[128,128]{1,0:T(8,128)S(1)} %copy-done.1, f32[128,128]{1,0:T(8,128)S(1)} %copy-done.2, f32[1,128]{1,0:T(1,128)S(1)} %broadcast_in_dim_tile.3.k_ref, f32[3]{0:T(128)S(1)} %copy-done.3), custom_call_target="tpu_custom_call" | custom-call | tf_op jit(solution)/shard_map/krylov/pallas_call | solution.py:598
  89.2 0.9 copy.7
Async XLA Ops:
  0.7 0.7 copy-start.3
  1.3 1.1 %copy-start = (f32[3,32,8,256]{3,2,1,0:T(8,128)S(1)}, f32[3,32,8,256]{3,2,1,0:T(8,128)}, u32[]{:S(2)}) copy-start(f32[3,32,8,256]{3,2,1,0:T(8,128)} %x_ref.1) | copy-start | bytes 2359300
  2.4 0.8 copy-start.1
  3.3 0.8 copy-start.2
